TPU v7x, 256 devices: a whole 4x4x8 slice. The times are simulated.
256 devices in a mesh: group: 8 (over z_hi, core), expert: 32 (over x, y, z_lo).
Axes of the slice: x: 4, y: 4, z: 8 (z_hi: 4, z_lo: 2; z = z_hi * 2 + z_lo), core: 2. Of those that a mesh axis runs over, the one named last changes fastest.
Arguments:
- dy_rows: bfloat16 [8, 32, 768, 3584], P('group', 'expert'), may hold values from -0.3125 to 0.3125
- hidden_rows: bfloat16 [8, 32, 768, 128], P('group', 'expert'), may hold values from -6 to 6
- row_counts: int32 [8, 32, 32, 2], P('group', 'expert'), may hold values from 0 to 24, as said below
- hot_owner: int32 [32], P('expert'), may hold values from 0 to 7
- master: float32 [8, 32, 128, 3584], P('group', 'expert'), may hold values from -0.5 to 0.5
- moment1: bfloat16 [8, 32, 128, 3584], P('group', 'expert'), may hold values from -1.796875 to 1.796875
- moment2: bfloat16 [8, 32, 128, 3584], P('group', 'expert'), may hold values from 0.019897461 to 0.5
Outputs:
- new_master: float32 [8, 32, 128, 3584], P('group', 'expert')
- new_moment1: bfloat16 [8, 32, 128, 3584], P('group', 'expert')
- new_moment2: bfloat16 [8, 32, 128, 3584], P('group', 'expert')
- replica_panel: bfloat16 [8, 32, 128, 3584], P('group', 'expert')
Inputs may be any that keep to these rules, and one draw needn't show every extreme that they name: row_counts[g, d, s, 0] + row_counts[g, d, s, 1] <= 24; the own rows come first in each block, then the hot rows; every receiving device has a block that is full.
All inputs are finite; a program needn't handle non-finite values.
Results may differ from a plain program's by a relative error of at most 0.0012.
Values may be sent and summed in bfloat16 or wider, within the bound.
A program may use at most 128 MiB of HBM per device.

v0:
```python
import jax
import jax.numpy as jnp
from jax import lax
from jax.sharding import PartitionSpec as P

beta_one = 0.9
beta_two = 0.95
learn_rate = 0.00022
weight_decay = 0.1
epsilon = 1e-08
bias_one = 1.0 - 0.9**10
bias_two = 1.0 - 0.95**10


def spread(array, axis, root):
    mine = lax.axis_index(axis) == root
    return lax.psum(jnp.where(mine, array, jnp.zeros_like(array)), axis)


def adamw_update(master, moment1, moment2, gradient):
    first_moment = beta_one * moment1.astype(jnp.float32) + (1.0 - beta_one) * gradient
    second_moment = beta_two * moment2.astype(jnp.float32) + (1.0 - beta_two) * gradient * gradient
    direction = first_moment / bias_one / (jnp.sqrt(second_moment / bias_two) + epsilon)
    updated = master * (1.0 - learn_rate * weight_decay) - learn_rate * direction
    return (updated, first_moment.astype(jnp.bfloat16), second_moment.astype(jnp.bfloat16))


def slot_masks(counts, cap_rows):
    position = jnp.arange(cap_rows, dtype=jnp.int32)
    lower = counts[..., 0:1]
    upper = lower + counts[..., 1:2]
    return (position < lower, (position >= lower) & (position < upper))


def weight_term(hidden, mask, received):
    chosen = jnp.where(mask[:, None], hidden, jnp.zeros_like(hidden))
    return lax.dot_general(
        chosen, received, (((0,), (0,)), ((), ())), preferred_element_type=jnp.float32
    )


def local(dy_rows, hidden_rows, row_counts, hot_owner, master, moment1, moment2):
    owner_group = hot_owner[0]
    received = lax.all_to_all(dy_rows, "expert", split_axis=2, concat_axis=2, tiled=True)[0, 0]
    counts = row_counts[0, 0]
    cap_rows = received.shape[0] // counts.shape[0]
    mask_own, mask_hot = slot_masks(counts, cap_rows)
    hidden = hidden_rows[0, 0]
    part_own = weight_term(hidden, mask_own.reshape(-1), received)
    part_hot = weight_term(hidden, mask_hot.reshape(-1), received)
    is_owner = lax.axis_index("group") == owner_group
    hot_term = part_hot + jnp.where(is_owner, part_own, 0.0)
    hot_total = lax.psum(hot_term, "group")
    gradient = jnp.where(is_owner, hot_total, part_own)
    new_master, new_moment1, new_moment2 = adamw_update(
        master[0, 0], moment1[0, 0], moment2[0, 0], gradient
    )
    replica = spread(new_master.astype(jnp.bfloat16), "group", owner_group)
    return (
        new_master[None, None],
        new_moment1[None, None],
        new_moment2[None, None],
        replica[None, None],
    )


def solution(mesh):
    return jax.shard_map(
        local,
        mesh=mesh,
        in_specs=(
            P("group", "expert", None, None),
            P("group", "expert", None, None),
            P("group", "expert", None, None),
            P("expert"),
            P("group", "expert", None, None),
            P("group", "expert", None, None),
            P("group", "expert", None, None),
        ),
        out_specs=(
            P("group", "expert", None, None),
            P("group", "expert", None, None),
            P("group", "expert", None, None),
            P("group", "expert", None, None),
        ),
        check_vma=False,
    )
```

profile of v0, /device:TPU:7, one launch (start us, length us, event | category | flops | bytes accessed | tf_op | source)
XLA Modules:
  0.0 369.0 jit_solution(190936308283983087)
XLA Ops:
  7.2 10.9 %copy.23 = bf16[1,1,768,3584]{3,1,0,2:T(2,128)(2,1)} copy(bf16[1,1,768,3584]{3,2,1,0:T(8,128)(2,1)} %param.7) | data formatting | bytes 11010048 | tf_op args[0]
  18.0 0.5 broadcast.40
  18.6 36.8 %reduce = bf16[768,3584]{1,0:T(8,128)(2,1)} reduce(bf16[768,1,1,3584]{3,2,1,0:T(2,128)(2,1)} %bitcast.52, bf16[]{:T(256)} %broadcast.40), dimensions={1,2}, to_apply=%bitcast.50.reduce_sub_computation | reduce | bytes 11010050
  55.3 13.3 %reshape.76 = bf16[32,2,43008]{2,1,0:T(2,128)(2,1)} reshape(bf16[768,3584]{1,0:T(8,128)(2,1)} %reduce) | data formatting | bytes 11010048
  68.7 0.0 copy-start.2
  68.7 8.6 %all-to-all-start = ((bf16[32,2,43008]{2,1,0:T(2,128)(2,1)}), bf16[32,2,43008]{2,1,0:T(2,128)(2,1)}, u32[]{:S(2)}, u32[]{:S(2)}) async-start(bf16[32,2,43008]{2,1,0:T(2,128)(2,1)} %reshape.76), calls=%async_computation | async-start | bytes 11010048 | tf_op jit(solution)/shard_map/all_to_all | solution.py:44
  77.2 0.0 all-reduce.3.cloned.1.call-start
  78.0 0.0 copy-done.2
  78.0 0.1 fusion.22
  78.1 0.1 lt.38
  78.2 0.1 and.12
  78.3 0.0 copy-start.1
  78.3 86.2 %all-to-all-done = bf16[32,2,43008]{2,1,0:T(2,128)(2,1)} async-done(((bf16[32,2,43008]{2,1,0:T(2,128)(2,1)}), bf16[32,2,43008]{2,1,0:T(2,128)(2,1)}, u32[]{:S(2)}, u32[]{:S(2)}) %all-to-all-start) | async-done | bytes 5505056 | tf_op jit(solution)/shard_map/all_to_all | solution.py:44
  164.4 20.9 %reshape.77 = bf16[768,1,1,3584]{3,2,1,0:T(2,128)(2,1)} reshape(bf16[32,2,43008]{2,1,0:T(2,128)(2,1)} %all-to-all-done) | data formatting | bytes 11010048
  185.4 0.0 copy-done.1
  185.4 5.1 %fusion = f32[128,3584]{1,0:T(8,128)S(1)} fusion(bf16[1,1,768,3584]{3,1,0,2:T(2,128)(2,1)} %bitcast.53, bf16[1,1,768,128]{3,2,1,0:T(8,128)(2,1)S(1)} %copy-done.1, pred[768]{0:T(1024)(128)(4,1)S(1)} %lt.38), kind=kOutput, calls=%fused_computation | convolution fusion | flops 704741376 | bytes 7537408 | tf_op jit(solution)/shard_map/dot_general | solution.py:37
  190.5 6.4 %fusion.4 = f32[128,3584]{1,0:T(8,128)} fusion(bf16[1,1,768,3584]{3,1,0,2:T(2,128)(2,1)} %bitcast.54, f32[128,3584]{1,0:T(8,128)S(1)} %fusion, pred[]{:T(512)S(6)} %eq.4, bf16[1,1,768,128]{3,2,1,0:T(8,128)(2,1)S(1)} %copy-done.1, pred[768]{0:T(1024)(128)(4,1)S(1)} %and.12), kind=kOutput, calls=%fused_computation.4 | convolution fusion | flops 705658880 | bytes 9372417 | tf_op jit(solution)/shard_map/dot_general | solution.py:37
  196.9 0.0 copy-start
  196.9 0.0 all-reduce.3.cloned.1.call-update
  196.9 0.0 all-reduce.5.cloned.1.call-start
  197.0 81.6 %all-reduce.3.cloned.1.call-done = f32[128,3584]{1,0:T(8,128)} async-done(((f32[128,3584]{1,0:T(8,128)}), f32[128,3584]{1,0:T(8,128)}) %all-reduce.3.cloned.1.call-update) | async-done | bytes 1835024 | tf_op jit(solution)/shard_map/psum | solution.py:53
  278.5 0.0 copy-done
  278.5 5.7 %select_bitcast_fusion = (bf16[1,1,128,3584]{3,2,1,0:T(8,128)(2,1)}, f32[128,3584]{1,0:T(8,128)}, f32[128,3584]{1,0:T(8,128)}) fusion(pred[]{:T(512)S(6)} %eq.4, bf16[1,1,128,3584]{3,2,1,0:T(8,128)(2,1)S(1)} %copy-done, bf16[1,1,128,3584]{3,2,1,0:T(8,128)(2,1)} %param.12, f32[1,1,128,3584]{3,2,1,0:T(8,128)} %param.11, ...), kind=kLoop, calls=%fused_computation.15 | loop fusion | flops 8716288 | bytes 11927553 | tf_op jit(solution)/shard_map/broadcast_in_dim | solution.py:63
  284.2 0.0 all-reduce.5.cloned.1.call-update
  284.2 3.6 fusion.12
  287.8 72.2 %all-reduce.5.cloned.1.call-done = bf16[1,1,128,3584]{3,2,1,0:T(8,128)(2,1)} async-done(((bf16[1,1,128,3584]{3,2,1,0:T(8,128)(2,1)}), bf16[1,1,128,3584]{3,2,1,0:T(8,128)(2,1)}) %all-reduce.5.cloned.1.call-update) | async-done | bytes 917520 | tf_op jit(solution)/shard_map/psum | solution.py:17
  360.0 2.2 copy.27
  (1 shorter events, 0.0 us)
Async XLA Ops:
  68.7 9.3 %copy-start.2 = (s32[1,1,32,2]{2,3,1,0:T(2,128)S(1)}, s32[1,1,32,2]{2,3,1,0:T(2,128)}, u32[]{:S(2)}) copy-start(s32[1,1,32,2]{2,3,1,0:T(2,128)} %param.9) | copy-start | bytes 772
  68.7 95.8 %all-to-all-start = ((bf16[32,2,43008]{2,1,0:T(2,128)(2,1)}), bf16[32,2,43008]{2,1,0:T(2,128)(2,1)}, u32[]{:S(2)}, u32[]{:S(2)}) async-start(bf16[32,2,43008]{2,1,0:T(2,128)(2,1)} %reshape.76), calls=%async_computation | async-start | bytes 11010048 | tf_op jit(solution)/shard_map/all_to_all | solution.py:44
  77.2 201.3 %all-reduce.3.cloned.1.call-start = ((), (), s32[]{:S(2)}) async-start(), calls=%async_computation.1 | async-start | bytes 3670016 | tf_op jit(solution)/shard_map/psum | solution.py:53
  78.3 107.1 %copy-start.1 = (bf16[1,1,768,128]{3,2,1,0:T(8,128)(2,1)S(1)}, bf16[1,1,768,128]{3,2,1,0:T(8,128)(2,1)}, u32[]{:S(2)}) copy-start(bf16[1,1,768,128]{3,2,1,0:T(8,128)(2,1)} %param.8) | copy-start | bytes 589828
  196.9 81.7 %copy-start = (bf16[1,1,128,3584]{3,2,1,0:T(8,128)(2,1)S(1)}, bf16[1,1,128,3584]{3,2,1,0:T(8,128)(2,1)}, u32[]{:S(2)}) copy-start(bf16[1,1,128,3584]{3,2,1,0:T(8,128)(2,1)} %param.13) | copy-start | bytes 2752516
  196.9 163.1 %all-reduce.5.cloned.1.call-start = ((), (), s32[]{:S(2)}) async-start(), calls=%async_computation.2 | async-start | bytes 1835008 | tf_op jit(solution)/shard_map/psum | solution.py:17
Sparse Core Ops, SparseCore 0:
  197.0 81.4 all-reduce.2
  284.4 75.6 all-reduce.4
where the time goes:
time: 371 us; the launch traced here: 369 us
  waiting for transfers between devices  240 us (65%)
  local copies, waits for them, and re-layouts  48 us (13%)
  other arithmetic  46.1 us (12%)
  between operations  14.7 us (4%)
  matrix products  11.5 us (3%)
  starting transfers between devices  8.66 us (2%)
    all_to_all x1, waiting for transfers between devices, local(): lax.all_to_all(dy_rows, 'expert', split_axis=2, concat_axis=2, tiled=True)  86.2 us
    psum x1, waiting for transfers between devices, local(): hot_total = lax.psum(hot_term, 'group')  81.6 us
    psum x1, waiting for transfers between devices, spread(): return lax.psum(jnp.where(mine, array, jnp.zeros_like(array)), axis)  72.2 us
    unnamed x11, local copies, waits for them, and re-layouts  47.8 us
    unnamed x1, other arithmetic  36.8 us
    dot_general x2, matrix products, weight_term(): lax.dot_general(chosen, received, (((0,), (0,)), ((), ())), preferred_ele...  11.5 us
    all_to_all x1, starting transfers between devices, local(): lax.all_to_all(dy_rows, 'expert', split_axis=2, concat_axis=2, tiled=True)  8.58 us
  transfers between devices with their start and end apart: 3, of which 3 were waited for; matrix products, arithmetic and copies ran while one was open for 1% of the time, Pallas kernels for 0%

commit v1 on v0

v1 whole, which is shorter than its diff:
```python
import functools

import jax
import jax.numpy as jnp
from jax import lax
from jax.experimental import pallas as pl
from jax.experimental.pallas import tpu as pltpu
from jax.sharding import PartitionSpec as P

MESH = pl.DeviceIdType.MESH
F32, BF16 = jnp.float32, jnp.bfloat16

beta_one = 0.9
beta_two = 0.95
learn_rate = 0.00022
weight_decay = 0.1
epsilon = 1e-08
bias_one = 1.0 - 0.9**10
bias_two = 1.0 - 0.95**10

ROWS, HID, WIN, CAP = 768, 128, 3584, 24
WIDTHS = (512,) * 7
SPACING = 4
AHEAD = 2


def kernel(
    dy, hid, cnt, owner, master, moment1, moment2,
    out_master, out_m1, out_m2, out_rep,
    recv, hidden, hidden_f, left_f, left, x_out, x_in,
    prod, own_in, sib_in, rs_in, total, mst, m1, m2, rep, rep_in, rep_slices, rep_full,
    s_in, s_x, s_a, s_own, s_sib, s_rs, s_ag, s_fwd, s_g1, s_g2, s_g3, s_g4, s_out,
):
    g, e = lax.axis_index("group"), lax.axis_index("expert")
    zh, c = lax.div(g, 2), lax.rem(g, 2)
    xy, p = lax.div(e, 2), lax.rem(e, 2)
    x, y = lax.div(xy, 4), lax.rem(xy, 4)
    z = 2 * zh + p
    o = lax.rem(p + c, 2)
    sigma = 1 - 2 * c
    partner = (g, e + 1 - 2 * p)
    sibling = (g + 1 - 2 * c, e)

    def ring(step):
        zz = lax.rem(z + step + 8, 8)
        return (lax.div(zz, 2) * 2 + c, xy * 2 + lax.rem(zz, 2))

    def column(i):
        return lax.rem(zh + i, 4)

    def plane(dx, dy_):
        return lax.rem(x + dx, 4) * 4 + lax.rem(y + dy_, 4)

    starts = [sum(WIDTHS[:k]) for k in range(len(WIDTHS))]
    count = len(WIDTHS)
    cols = [pl.ds(s, w) for s, w in zip(starts, WIDTHS)]
    offsets = [(a, b) for a in range(4) for b in range(4) if (a, b) != (0, 0)]

    def remote(src, dst, sems, device):
        return pltpu.make_async_remote_copy(
            src_ref=src, dst_ref=dst, send_sem=sems[0], recv_sem=sems[1],
            device_id=device, device_id_type=MESH,
        )

    def pair(sems, *index):
        return sems.at[(0, *index)], sems.at[(1, *index)]

    loads = [
        pltpu.make_async_copy(hid.at[0, 0], hidden, s_in.at[0]),
        pltpu.make_async_copy(master.at[0, 0], mst, s_in.at[1]),
        pltpu.make_async_copy(moment1.at[0, 0], m1, s_in.at[2]),
        pltpu.make_async_copy(moment2.at[0, 0], m2, s_in.at[3]),
    ]
    for load in loads:
        load.start()

    barrier = pltpu.get_barrier_semaphore()
    peers = [(g, plane(a, b) * 2 + p) for a, b in offsets]
    peers += [sibling, ring(1), ring(-1)]
    peers += [(column(i) * 2 + c, e) for i in (1, 2, 3)]
    for peer in peers:
        pl.semaphore_signal(barrier, inc=1, device_id=peer, device_id_type=MESH)
    pl.semaphore_wait(barrier, len(peers))

    def rows_start(k):
        for a, b in offsets:
            there = plane(a, b)
            remote(
                dy.at[0, 0, pl.ds(pl.multiple_of(there * 48, 48), 48), cols[k]],
                recv.at[xy, :, cols[k]],
                pair(s_a, k),
                (g, there * 2 + p),
            ).start()
        pltpu.make_async_copy(
            dy.at[0, 0, pl.ds(pl.multiple_of(xy * 48, 48), 48), cols[k]],
            recv.at[xy, :, cols[k]],
            s_a.at[1, k],
        ).start()

    for k in range(min(AHEAD + 1, count)):
        rows_start(k)

    loads[0].wait()
    hidden_f[...] = hidden[...].astype(F32)
    left_f[...] = jnp.zeros_like(left_f)
    position = lax.broadcasted_iota(jnp.int32, (CAP, HID), 0)
    owns = owner[0] == g

    def masked(s):
        h = hidden_f[pl.ds(pl.multiple_of(s * CAP, 8), CAP), :]
        a = cnt[0, 0, s, 0]
        upper = a + cnt[0, 0, s, 1]
        lower = jnp.where(owns, 0, a)
        own = jnp.where(position < a, h, 0.0)
        hot = jnp.where((position >= lower) & (position < upper), h, 0.0)
        return own, hot

    def fill_out(i, carry):
        own, hot = masked(2 * i + 1 - p)
        at = pl.ds(pl.multiple_of(i * CAP, 8), CAP)
        x_out_f = left_f
        x_out_f[at, 0:HID] = own
        x_out_f[at, HID : 2 * HID] = hot
        return carry

    lax.fori_loop(0, 16, fill_out, 0)
    x_out[...] = left_f[0:384, 0:256].astype(BF16)
    send_x = remote(x_out, x_in, (s_x.at[0], s_x.at[1]), partner)
    send_x.start()
    left_f[...] = jnp.zeros_like(left_f)

    def fill_mine(i, carry):
        own, hot = masked(2 * i + p)
        at = pl.ds(pl.multiple_of(i * 48 + p * CAP, 8), CAP)
        left_f[at, 0:HID] = own
        left_f[at, 2 * HID : 3 * HID] = hot
        return carry

    lax.fori_loop(0, 16, fill_mine, 0)
    send_x.wait_recv()
    hidden_x = hidden_f
    for half in range(2):
        hidden_x[0:384, :] = x_in[:, half * HID : (half + 1) * HID].astype(F32)

        def fill_other(i, carry):
            at = pl.ds(pl.multiple_of(i * 48 + (1 - p) * CAP, 8), CAP)
            block = hidden_x[pl.ds(pl.multiple_of(i * CAP, 8), CAP), :]
            left_f[at, (2 * half + 1) * HID : (2 * half + 2) * HID] = block
            return carry

        lax.fori_loop(0, 16, fill_other, 0)
    for j in range(4):
        left[j * HID : (j + 1) * HID, :] = left_f[:, j * HID : (j + 1) * HID].T.astype(BF16)

    def rows_of(delta):
        home = lax.rem(z - sigma * delta + 16, 8)
        return pl.ds(pl.multiple_of(lax.div(home - c, 2) * 32, 32), 32)

    hot_mine = pl.ds(pl.multiple_of(2 * HID + HID * o, HID), HID)
    hot_other = pl.ds(pl.multiple_of(2 * HID + HID * (1 - o), HID), HID)
    here = pl.ds(pl.multiple_of(zh * 32, 32), 32)

    def own_copy(k):
        return remote(prod.at[HID : 2 * HID, cols[k]], own_in.at[:, cols[k]], pair(s_own, k), partner)

    def sib_copy(k):
        return remote(prod.at[hot_other, cols[k]], sib_in.at[:, cols[k]], pair(s_sib, k), sibling)

    toward = sigma * (2 * o - 1)

    def rs_copy(k, step):
        direction = (toward, -toward, toward, -sigma)[step]
        src = sib_in.at[rows_of(4 + o), cols[k]] if step == 0 else rs_in.at[step - 1, :, cols[k]]
        return remote(src, rs_in.at[step, :, cols[k]], pair(s_rs, k, step), ring(direction))

    def ag_copy(k, i):
        return remote(total.at[here, cols[k]], total.at[here, cols[k]], pair(s_ag, k, i - 1), (column(i) * 2 + c, e))

    def fwd_copy(k):
        return remote(total.at[:, cols[k]], total.at[:, cols[k]], pair(s_fwd, k), sibling)

    def g1_copy(k):
        return remote(rep.at[:, cols[k]], rep_in.at[:, cols[k]], pair(s_g1, k), sibling)

    def g2_copy(k, i):
        there = pl.ds(pl.multiple_of(column(i) * 32, 32), 32)
        return remote(rep.at[there, cols[k]], rep_slices.at[i - 1, :, cols[k]], pair(s_g2, k, i - 1), (column(i) * 2 + c, e))

    def g3_copy(k, i):
        return remote(rep_full.at[here, cols[k]], rep_full.at[here, cols[k]], pair(s_g3, k, i - 1), (column(i) * 2 + c, e))

    def g4_copy(k):
        return remote(rep_full.at[:, cols[k]], rep_full.at[:, cols[k]], pair(s_g4, k), sibling)

    def out_copy(k, n):
        src = (mst, m1, m2, rep_full)[n]
        dst = (out_master, out_m1, out_m2, out_rep)[n]
        return pltpu.make_async_copy(src.at[:, cols[k]], dst.at[0, 0, :, cols[k]], s_out.at[k, n])

    def product(k):
        pltpu.make_async_copy(recv.at[:, :, cols[k]], recv.at[:, :, cols[k]], s_a.at[1, k]).wait()
        if k + AHEAD + 1 < count:
            rows_start(k + AHEAD + 1)

        def block(n, carry):
            at = pl.ds(pl.multiple_of(starts[k] + n * 256, 256), 256)
            right = recv[:, :, at].reshape(ROWS, 256)
            for j in range(2):
                rows = pl.ds(j * 256, 256)
                prod[rows, at] = jnp.dot(left[rows, :], right, preferred_element_type=F32)
            return carry

        lax.fori_loop(0, WIDTHS[k] // 256, block, 0)
        sib_copy(k).start()
        own_copy(k).start()

    def chip_sum(k):
        sib_copy(k).wait_recv()
        sib_in[:, cols[k]] += prod[hot_mine, cols[k]]
        rs_copy(k, 0).start()

    def relay(step, delta):
        def run(k):
            rs_copy(k, step - 1).wait_recv()
            rs_in[step - 1, :, cols[k]] += sib_in[rows_of(delta), cols[k]]
            rs_copy(k, step).start()

        return run

    def last_relay(k):
        @pl.when(o == 1)
        def _():
            relay(3, 1)(k)

    def gather(k):
        @pl.when(o == 0)
        def _():
            rs_copy(k, 2).wait_recv()
            rs_copy(k, 3).wait_recv()
            total[here, cols[k]] = sib_in[here, cols[k]] + rs_in[2, :, cols[k]] + rs_in[3, :, cols[k]]
            for i in (2, 1, 3):
                ag_copy(k, i).start()

    def ag_wait(k, i, buffer, sems):
        there = pl.ds(pl.multiple_of(lax.rem(zh + 4 - i, 4) * 32, 32), 32)
        remote(buffer.at[there, cols[k]], buffer.at[there, cols[k]], pair(sems, k, i - 1), sibling).wait_recv()

    def forward(k):
        @pl.when(o == 0)
        def _():
            for i in (1, 3, 2):
                ag_wait(k, i, total, s_ag)
            fwd_copy(k).start()

    def update(k):
        if k == 0:
            for load in loads[1:]:
                load.wait()

        @pl.when(o == 1)
        def _():
            fwd_copy(k).wait_recv()

        own_copy(k).wait_recv()
        w = WIDTHS[k]

        def block(n, carry):
            at = (pl.ds(pl.multiple_of(n * 16, 16), 16), cols[k])
            mask = jnp.full((16, w), owner[0], jnp.int32) == jnp.full((16, w), g, jnp.int32)
            gradient = jnp.where(mask, total[at], prod[at] + own_in[at])
            first = beta_one * m1[at].astype(F32) + (1.0 - beta_one) * gradient
            second = beta_two * m2[at].astype(F32) + (1.0 - beta_two) * gradient * gradient
            direction = first / (bias_one * (jnp.sqrt(second * (1.0 / bias_two)) + epsilon))
            updated = mst[at] * (1.0 - learn_rate * weight_decay) - learn_rate * direction
            mst[at] = updated
            m1[at] = first.astype(BF16)
            m2[at] = second.astype(BF16)
            rep[at] = jnp.where(mask, updated, 0.0).astype(BF16)
            return carry

        lax.fori_loop(0, 8, block, 0)

        @pl.when(o == 1)
        def _():
            g1_copy(k).start()

        for n in range(3):
            out_copy(k, n).start()

    def scatter(k):
        @pl.when(o == 0)
        def _():
            g1_copy(k).wait_recv()
            rep[:, cols[k]] += rep_in[:, cols[k]]
            for i in (2, 1, 3):
                g2_copy(k, i).start()

    def regather(k):
        @pl.when(o == 0)
        def _():
            for i in (1, 3, 2):
                g2_copy(k, i).wait_recv()
            rep_full[here, cols[k]] = (rep[here, cols[k]] + rep_slices[0, :, cols[k]]) + (
                rep_slices[1, :, cols[k]] + rep_slices[2, :, cols[k]]
            )
            for i in (2, 1, 3):
                g3_copy(k, i).start()

    def share(k):
        @pl.when(o == 0)
        def _():
            for i in (1, 3, 2):
                ag_wait(k, i, rep_full, s_g3)
            g4_copy(k).start()

    def finish(k):
        @pl.when(o == 1)
        def _():
            g4_copy(k).wait_recv()

        out_copy(k, 3).start()

    stages = [
        product, chip_sum, relay(1, 6 - 3 * o), relay(2, 2 + 5 * o), last_relay, gather,
        forward, update, scatter, regather, share, finish,
    ]
    order = sorted(
        (SPACING * k + i, -k, i) for k in range(count) for i in range(len(stages))
    )
    for _, minus, i in order:
        stages[i](-minus)

    send_x.wait_send()
    for k in range(count):
        half = recv.at[0:15, :, cols[k]]
        remote(half, half, pair(s_a, k), sibling).wait_send()
        own_copy(k).wait_send()
        sib_copy(k).wait_send()
        for step in range(3):
            rs_copy(k, step).wait_send()

        @pl.when(o == 1)
        def _():
            rs_copy(k, 3).wait_send()
            g1_copy(k).wait_send()

        @pl.when(o == 0)
        def _():
            for i in (1, 2, 3):
                ag_copy(k, i).wait_send()
                g2_copy(k, i).wait_send()
                g3_copy(k, i).wait_send()
            fwd_copy(k).wait_send()
            g4_copy(k).wait_send()

        for n in range(4):
            out_copy(k, n).wait()


def local(dy_rows, hidden_rows, row_counts, hot_owner, master, moment1, moment2):
    count = len(WIDTHS)
    dma = pltpu.SemaphoreType.DMA
    anywhere = pl.BlockSpec(memory_space=pl.ANY)
    scalars = pl.BlockSpec(memory_space=pltpu.SMEM)
    return pl.pallas_call(
        kernel,
        name="expert_grad",
        out_shape=(
            jax.ShapeDtypeStruct((1, 1, HID, WIN), F32),
            jax.ShapeDtypeStruct((1, 1, HID, WIN), BF16),
            jax.ShapeDtypeStruct((1, 1, HID, WIN), BF16),
            jax.ShapeDtypeStruct((1, 1, HID, WIN), BF16),
        ),
        in_specs=[anywhere, anywhere, scalars, scalars, anywhere, anywhere, anywhere],
        out_specs=(anywhere,) * 4,
        scratch_shapes=[
            pltpu.VMEM((16, 48, WIN), BF16),
            pltpu.VMEM((ROWS, HID), BF16),
            pltpu.VMEM((ROWS, HID), F32),
            pltpu.VMEM((ROWS, 4 * HID), F32),
            pltpu.VMEM((4 * HID, ROWS), BF16),
            pltpu.VMEM((ROWS // 2, 2 * HID), BF16),
            pltpu.VMEM((ROWS // 2, 2 * HID), BF16),
            pltpu.VMEM((4 * HID, WIN), F32),
            pltpu.VMEM((HID, WIN), F32),
            pltpu.VMEM((HID, WIN), F32),
            pltpu.VMEM((4, 32, WIN), F32),
            pltpu.VMEM((HID, WIN), F32),
            pltpu.VMEM((HID, WIN), F32),
            pltpu.VMEM((HID, WIN), BF16),
            pltpu.VMEM((HID, WIN), BF16),
            pltpu.VMEM((HID, WIN), BF16),
            pltpu.VMEM((HID, WIN), BF16),
            pltpu.VMEM((3, 32, WIN), BF16),
            pltpu.VMEM((HID, WIN), BF16),
            dma((4,)),
            dma((2,)),
            dma((2, count)),
            dma((2, count)),
            dma((2, count)),
            dma((2, count, 4)),
            dma((2, count, 3)),
            dma((2, count)),
            dma((2, count)),
            dma((2, count, 3)),
            dma((2, count, 3)),
            dma((2, count)),
            dma((count, 4)),
        ],
        compiler_params=pltpu.CompilerParams(
            collective_id=0, has_side_effects=True, vmem_limit_bytes=56 * 2**20
        ),
        cost_estimate=pl.CostEstimate(
            flops=2 * 4 * HID * ROWS * WIN, bytes_accessed=16 * 2**20, transcendentals=HID * WIN
        ),
    )(dy_rows, hidden_rows, row_counts, hot_owner, master, moment1, moment2)


def solution(mesh):
    rows = P("group", "expert", None, None)
    return jax.shard_map(
        local,
        mesh=mesh,
        in_specs=(rows, rows, rows, P("expert"), rows, rows, rows),
        out_specs=(rows,) * 4,
        check_vma=False,
    )
```

time: 371 us -> 183 us (0.49)
  waiting for transfers between devices: 240 us -> 0 us
  Pallas kernels: 0 us -> 175 us
  other arithmetic: 46.1 us -> 0 us
  local copies, waits for them, and re-layouts: 48 us -> 7.14 us
  between operations: 14.7 us -> 1.31 us
  matrix products: 11.5 us -> 0 us
  starting transfers between devices: 8.66 us -> 0 us
    pallas_call x0 -> x1, Pallas kernels: none -> 175 us  [local(): pl.pallas_call(kernel, name='expert_grad', out_shape=(jax.ShapeDtypeStruc...]
    psum x2 -> x0, waiting for transfers between devices: 154 us -> none  [the longest x1 81.6 us: local(): hot_total = lax.psum(hot_term, 'group')]
    all_to_all x1 -> x0, waiting for transfers between devices: 86.2 us -> none  [local(): lax.all_to_all(dy_rows, 'expert', split_axis=2, concat_axis=2, tiled=True)]
    unnamed x11, local copies, waits for them, and re-layouts: 47.8 us -> 7.14 us
    unnamed x1 -> x0, other arithmetic: 36.8 us -> none
    dot_general x2 -> x0, matrix products: 11.5 us -> none  [weight_term(): lax.dot_general(chosen, received, (((0,), (0,)), ((), ())), preferred_ele...]
    broadcast_in_dim x2 -> x0, other arithmetic: 9.22 us -> none  [the longest x1 5.67 us: local(): replica[None, None]]
    all_to_all x1 -> x0, starting transfers between devices: 8.58 us -> none  [local(): lax.all_to_all(dy_rows, 'expert', split_axis=2, concat_axis=2, tiled=True)]
  transfers between devices with their start and end apart: 3 -> 0, of which waited for: 3 -> 0; matrix products, arithmetic and copies ran while one was open for 1% -> 0% of each run, Pallas kernels for 0% -> 0%
where the time goes in v1:
time: 183 us
  Pallas kernels  175 us (96%)
  local copies, waits for them, and re-layouts  7.14 us (4%)
    pallas_call x1, Pallas kernels, local(): pl.pallas_call(kernel, name='expert_grad', out_shape=(jax.ShapeDtypeStruc...  175 us
    unnamed x11, local copies, waits for them, and re-layouts  7.14 us

profile of v1, /device:TPU:7, one launch (start us, length us, event | category | flops | bytes accessed | tf_op | source)
XLA Modules:
  0.0 183.2 jit_solution(368856093878958375)
XLA Ops:
  1.3 1.4 copy.11.cnt
  2.6 174.7 %expert_grad.1 = (f32[1,1,128,3584]{3,2,1,0:T(8,128)}, bf16[1,1,128,3584]{3,2,1,0:T(8,128)(2,1)}, bf16[1,1,128,3584]{3,2,1,0:T(8,128)(2,1)}, bf16[1,1,128,3584]{3,2,1,0:T(8,128)(2,1)}) custom-call(bf16[1,1,768,3584]{3,2,1,0:T(8,128)(2,1)} %dy.1, bf16[1,1,768,128]{3,2,1,0:T(8,128)(2,1)} %hid.1, s32[1,1,32,2]{3,2,1,0:T(8,128)} %copy.11.cnt, s32[1]{0:T(128)S(6)} %copy.16.owner, ...), custom_call_target="tpu_custom_call" | custom-call | flops 2818572288 | bytes 16777216 | tf_op jit(solution)/shard_map/expert_grad/pallas_call | solution.py:365
  177.4 0.0 copy-start.2
  177.4 0.0 copy-start.1
  177.4 3.0 %copy.17 = f32[1,1,128,3584]{3,2,1,0:T(8,128)} copy(f32[1,1,128,3584]{3,2,1,0:T(8,128)} %get-tuple-element.8) | data formatting | bytes 3670016
  180.4 0.0 copy-done.2
  180.4 0.0 copy-start
  180.4 0.9 copy.18
  181.3 0.0 copy-done.1
  181.3 0.9 copy.19
  182.2 0.0 copy-done
  182.2 0.9 copy.20
Async XLA Ops:
  177.4 3.0 %copy-start.2 = (bf16[1,1,128,3584]{3,2,1,0:T(8,128)(2,1)S(1)}, bf16[1,1,128,3584]{3,2,1,0:T(8,128)(2,1)}, u32[]{:S(2)}) copy-start(bf16[1,1,128,3584]{3,2,1,0:T(8,128)(2,1)} %get-tuple-element.9) | copy-start | bytes 2752516
  177.4 3.9 %copy-start.1 = (bf16[1,1,128,3584]{3,2,1,0:T(8,128)(2,1)S(1)}, bf16[1,1,128,3584]{3,2,1,0:T(8,128)(2,1)}, u32[]{:S(2)}) copy-start(bf16[1,1,128,3584]{3,2,1,0:T(8,128)(2,1)} %get-tuple-element.10) | copy-start | bytes 2752516
  180.4 1.9 %copy-start = (bf16[1,1,128,3584]{3,2,1,0:T(8,128)(2,1)S(1)}, bf16[1,1,128,3584]{3,2,1,0:T(8,128)(2,1)}, u32[]{:S(2)}) copy-start(bf16[1,1,128,3584]{3,2,1,0:T(8,128)(2,1)} %get-tuple-element.11) | copy-start | bytes 2752516

commit v2 on v1

v2 whole, which is shorter than its diff:
```python
import functools

import jax
import jax.numpy as jnp
from jax import lax
from jax.experimental import pallas as pl
from jax.experimental.pallas import tpu as pltpu
from jax.sharding import PartitionSpec as P

MESH = pl.DeviceIdType.MESH
F32, BF16, I16 = jnp.float32, jnp.bfloat16, jnp.int16

beta_one = 0.9
beta_two = 0.95
learn_rate = 0.00022
weight_decay = 0.1
epsilon = 1e-08
bias_one = 1.0 - 0.9**10
bias_two = 1.0 - 0.95**10

ROWS, HID, WIN, CAP = 768, 128, 3584, 24
WIDTHS = (256,) * 14
SPACING = 1
NEWEST = 1
AHEAD = 2


def coded(value):
    peak = jnp.maximum(jnp.max(jnp.abs(value), axis=0, keepdims=True), 1e-30)
    code = jnp.round(value * (32767.0 / peak)).astype(jnp.int32).astype(jnp.int16)
    return code, peak * (1.0 / 32767.0)


def decoded(code, step):
    return code.astype(jnp.int32).astype(F32) * step


def kernel(
    dy, hid, cnt, owner, master, moment1, moment2,
    mst, m1, m2, rep_full,
    recv, hidden, hidden_f, left_f, left, x_out, x_in,
    prod, own_q, own_s, own_qi, own_si, sib_in, ring_q, ring_s, ring_qi, ring_si, rs_q, rs_s, rs_qi, rs_si, total_q, total_s,
    sib_mst, sib_m1, sib_m2, rep, rep_slices,
    s_in, s_state, s_x, s_a, s_own, s_sib, s_ring, s_rs, s_ag, s_fwd, s_g2, s_g3, s_g4,
):
    mst, m1, m2, rep_full = (ref.at[0, 0] for ref in (mst, m1, m2, rep_full))
    g, e = lax.axis_index("group"), lax.axis_index("expert")
    zh, c = lax.div(g, 2), lax.rem(g, 2)
    xy, p = lax.div(e, 2), lax.rem(e, 2)
    x, y = lax.div(xy, 4), lax.rem(xy, 4)
    z = 2 * zh + p
    o = lax.rem(p + c, 2)
    sigma = 1 - 2 * c
    partner = (g, e + 1 - 2 * p)
    sibling = (g + 1 - 2 * c, e)

    def ring(step):
        zz = lax.rem(z + step + 8, 8)
        return (lax.div(zz, 2) * 2 + c, xy * 2 + lax.rem(zz, 2))

    def column(i):
        return lax.rem(zh + i, 4)

    def plane(dx, dy_):
        return lax.rem(x + dx, 4) * 4 + lax.rem(y + dy_, 4)

    starts = [sum(WIDTHS[:k]) for k in range(len(WIDTHS))]
    count = len(WIDTHS)
    cols = [pl.ds(s, w) for s, w in zip(starts, WIDTHS)]
    offsets = [(a, b) for a in range(4) for b in range(4) if (a, b) != (0, 0)]

    def remote(src, dst, sems, device):
        return pltpu.make_async_remote_copy(
            src_ref=src, dst_ref=dst, send_sem=sems[0], recv_sem=sems[1],
            device_id=device, device_id_type=MESH,
        )

    def pair(sems, *index):
        return sems.at[(0, *index)], sems.at[(1, *index)]

    loads = [
        pltpu.make_async_copy(hid.at[0, 0], hidden, s_in.at[0]),
        pltpu.make_async_copy(master.at[0, 0], mst, s_in.at[1]),
        pltpu.make_async_copy(moment1.at[0, 0], m1, s_in.at[2]),
        pltpu.make_async_copy(moment2.at[0, 0], m2, s_in.at[3]),
    ]
    for load in loads:
        load.start()

    barrier = pltpu.get_barrier_semaphore()
    peers = [(g, plane(a, b) * 2 + p) for a, b in offsets]
    peers += [sibling, ring(1), ring(-1)]
    peers += [(column(i) * 2 + c, e) for i in (1, 2, 3)]
    for peer in peers:
        pl.semaphore_signal(barrier, inc=1, device_id=peer, device_id_type=MESH)
    pl.semaphore_wait(barrier, len(peers))

    def rows_start(k):
        for a, b in offsets:
            there = plane(a, b)
            remote(
                dy.at[0, 0, pl.ds(pl.multiple_of(there * 48, 48), 48), cols[k]],
                recv.at[xy, :, cols[k]],
                pair(s_a, k),
                (g, there * 2 + p),
            ).start()
        pltpu.make_async_copy(
            dy.at[0, 0, pl.ds(pl.multiple_of(xy * 48, 48), 48), cols[k]],
            recv.at[xy, :, cols[k]],
            s_a.at[1, k],
        ).start()

    rows_start(0)

    states = [
        remote(src.at[0, 0], dst, pair(s_state, n), sibling)
        for n, (src, dst) in enumerate(((master, sib_mst), (moment1, sib_m1), (moment2, sib_m2)))
    ]

    loads[0].wait()
    hidden_f[...] = hidden[...].astype(F32)
    left_f[...] = jnp.zeros_like(left_f)
    position = lax.broadcasted_iota(jnp.int32, (CAP, HID), 0)
    owns = owner[0] == g

    def masked(s):
        h = hidden_f[pl.ds(pl.multiple_of(s * CAP, 8), CAP), :]
        a = cnt[0, 0, 0, s]
        upper = a + cnt[0, 0, 1, s]
        lower = jnp.where(owns, 0, a)
        own = jnp.where(position < a, h, 0.0)
        hot = jnp.where((position >= lower) & (position < upper), h, 0.0)
        return own, hot

    def fill_out(i, carry):
        own, hot = masked(2 * i + 1 - p)
        at = pl.ds(pl.multiple_of(i * CAP, 8), CAP)
        x_out_f = left_f
        x_out_f[at, 0:HID] = own
        x_out_f[at, HID : 2 * HID] = hot
        return carry

    lax.fori_loop(0, 16, fill_out, 0)
    x_out[...] = left_f[0:384, 0:256].astype(BF16)
    send_x = remote(x_out, x_in, (s_x.at[0], s_x.at[1]), partner)
    send_x.start()
    for k in range(1, min(AHEAD + 1, count)):
        rows_start(k)
    @pl.when(o == 1)
    def _():
        for copy in states:
            copy.start()

    left_f[...] = jnp.zeros_like(left_f)

    def fill_mine(i, carry):
        own, hot = masked(2 * i + p)
        at = pl.ds(pl.multiple_of(i * 48 + p * CAP, 8), CAP)
        left_f[at, 0:HID] = own
        left_f[at, 2 * HID : 3 * HID] = hot
        return carry

    lax.fori_loop(0, 16, fill_mine, 0)
    send_x.wait_recv()
    hidden_x = hidden_f
    for half in range(2):
        hidden_x[0:384, :] = x_in[:, half * HID : (half + 1) * HID].astype(F32)

        def fill_other(i, carry):
            at = pl.ds(pl.multiple_of(i * 48 + (1 - p) * CAP, 8), CAP)
            block = hidden_x[pl.ds(pl.multiple_of(i * CAP, 8), CAP), :]
            left_f[at, (2 * half + 1) * HID : (2 * half + 2) * HID] = block
            return carry

        lax.fori_loop(0, 16, fill_other, 0)
    for j in range(4):
        left[j * HID : (j + 1) * HID, :] = left_f[:, j * HID : (j + 1) * HID].T.astype(BF16)

    hot_mine = pl.ds(pl.multiple_of(HID + HID * o, HID), HID)
    hot_other = pl.ds(pl.multiple_of(HID + HID * (1 - o), HID), HID)
    here = pl.ds(pl.multiple_of(zh * 32, 32), 32)

    def each(copies, what):
        for copy in copies:
            getattr(copy, what)()

    def own_copy(k):
        return (
            remote(own_q.at[:, cols[k]], own_qi.at[:, cols[k]], pair(s_own, k, 0), partner),
            remote(own_s.at[:, cols[k]], own_si.at[:, cols[k]], pair(s_own, k, 1), partner),
        )

    def sib_copy(k):
        return remote(prod.at[hot_other, cols[k]], sib_in.at[:, cols[k]], pair(s_sib, k), sibling)

    def rows_at(i):
        return pl.ds(pl.multiple_of(i * 32, 32), 32)

    def ring_copy(k):
        return (
            remote(ring_q.at[:, cols[k]], ring_qi.at[:, cols[k]], pair(s_ring, k, 0), ring(sigma)),
            remote(ring_s.at[:, cols[k]], ring_si.at[:, cols[k]], pair(s_ring, k, 1), ring(sigma)),
        )

    def rs_copy(k, i):
        j = column(i)
        there = (j * 2 + c, e)
        return (
            remote(rs_q.at[rows_at(j), cols[k]], rs_qi.at[i - 1, :, cols[k]], pair(s_rs, k, i - 1, 0), there),
            remote(rs_s.at[j, :, cols[k]], rs_si.at[i - 1, :, cols[k]], pair(s_rs, k, i - 1, 1), there),
        )

    def ag_copy(k, i):
        there = (column(i) * 2 + c, e)
        return (
            remote(total_q.at[here, cols[k]], total_q.at[here, cols[k]], pair(s_ag, k, i - 1, 0), there),
            remote(total_s.at[zh, :, cols[k]], total_s.at[zh, :, cols[k]], pair(s_ag, k, i - 1, 1), there),
        )

    def fwd_copy(k):
        return (
            remote(total_q.at[:, cols[k]], total_q.at[:, cols[k]], pair(s_fwd, k, 0), sibling),
            remote(total_s.at[:, :, cols[k]], total_s.at[:, :, cols[k]], pair(s_fwd, k, 1), sibling),
        )

    def g2_copy(k, i):
        there = pl.ds(pl.multiple_of(column(i) * 32, 32), 32)
        return remote(rep.at[there, cols[k]], rep_slices.at[i - 1, :, cols[k]], pair(s_g2, k, i - 1), (column(i) * 2 + c, e))

    def g3_copy(k, i):
        return remote(rep_full.at[here, cols[k]], rep_full.at[here, cols[k]], pair(s_g3, k, i - 1), (column(i) * 2 + c, e))

    def g4_copy(k):
        return remote(rep_full.at[:, cols[k]], rep_full.at[:, cols[k]], pair(s_g4, k), sibling)

    def tiles(k, body):
        wide = 256 if WIDTHS[k] % 256 == 0 else 128

        def block(n, carry):
            body(pl.ds(pl.multiple_of(starts[k] + n * wide, 128), wide))
            return carry

        lax.fori_loop(0, WIDTHS[k] // wide, block, 0)

    def product(k):
        pltpu.make_async_copy(recv.at[:, :, cols[k]], recv.at[:, :, cols[k]], s_a.at[1, k]).wait()
        if k + AHEAD + 1 < count:
            rows_start(k + AHEAD + 1)

        def body(at):
            right = recv[:, :, at].reshape(ROWS, at.size)
            own = jnp.dot(left[0 : 2 * HID, :], right, preferred_element_type=F32)
            prod[0:HID, at] = own[0:HID]
            own_q[:, at], own_s[:, at] = coded(own[HID:])
            prod[HID:, at] = jnp.dot(left[2 * HID :, :], right, preferred_element_type=F32)

        tiles(k, body)
        sib_copy(k).start()
        each(own_copy(k), "start")

    def chip_sum(k):
        sib_copy(k).wait_recv()
        sib_in[:, cols[k]] += prod[hot_mine, cols[k]]

        @pl.when(o == 1)
        def _():
            def body(at):
                ring_q[:, at], ring_s[:, at] = coded(sib_in[:, at])

            tiles(k, body)
            each(ring_copy(k), "start")

    def scatter(k):
        @pl.when(o == 0)
        def _():
            each(ring_copy(k), "wait_recv")

            def body(at):
                for j in range(4):
                    rows = pl.ds(j * 32, 32)
                    part = sib_in[rows, at] + decoded(ring_qi[rows, at], ring_si[:, at])
                    sib_in[rows, at] = part
                    rs_q[rows, at], rs_s[j, :, at] = coded(part)

            tiles(k, body)
            for i in (2, 1, 3):
                each(rs_copy(k, i), "start")

    def gather(k):
        @pl.when(o == 0)
        def _():
            for i in (1, 3, 2):
                each(rs_copy(k, i), "wait_recv")

            def body(at):
                part = sib_in[here, at]
                for i in range(3):
                    part = part + decoded(rs_qi[i, :, at], rs_si[i, :, at])
                total_q[here, at], total_s[zh, :, at] = coded(part)

            tiles(k, body)
            for i in (2, 1, 3):
                each(ag_copy(k, i), "start")

    def ag_wait(k, i, buffer, sems):
        there = pl.ds(pl.multiple_of(lax.rem(zh + 4 - i, 4) * 32, 32), 32)
        remote(buffer.at[there, cols[k]], buffer.at[there, cols[k]], pair(sems, k, i - 1), sibling).wait_recv()

    def adamw(old, first_old, second_old, gradient):
        first = beta_one * first_old.astype(F32) + (1.0 - beta_one) * gradient
        second = beta_two * second_old.astype(F32) + (1.0 - beta_two) * gradient * gradient
        direction = first / (bias_one * (jnp.sqrt(second * (1.0 / bias_two)) + epsilon))
        updated = old * (1.0 - learn_rate * weight_decay) - learn_rate * direction
        return updated, first.astype(BF16), second.astype(BF16)

    def belongs(group, w):
        return jnp.full((16, w), owner[0], jnp.int32) == jnp.full((16, w), group, jnp.int32)

    def blocks(k, body):
        def block(n, carry):
            at = (pl.ds(pl.multiple_of(n * 16, 16), 16), cols[k])
            body(at, decoded(total_q[at], total_s[lax.div(n, 2), :, cols[k]]))
            return carry

        lax.fori_loop(0, 8, block, 0)

    def replicate(k):
        if k == 0:
            for load in loads[1:]:
                load.wait()

        @pl.when(o == 0)
        def _():
            if k == 0:
                each(states, "wait_recv")
            for i in (1, 3, 2):
                frm = lax.rem(zh + 4 - i, 4)
                block = total_q.at[rows_at(frm), cols[k]]
                steps = total_s.at[frm, :, cols[k]]
                remote(block, block, pair(s_ag, k, i - 1, 0), sibling).wait_recv()
                remote(steps, steps, pair(s_ag, k, i - 1, 1), sibling).wait_recv()
            each(fwd_copy(k), "start")

            def body(at, hot):
                mine, other = belongs(g, WIDTHS[k]), belongs(sibling[0], WIDTHS[k])
                updated, _, _ = adamw(
                    jnp.where(mine, mst[at], sib_mst[at]),
                    jnp.where(mine, m1[at].astype(F32), sib_m1[at].astype(F32)),
                    jnp.where(mine, m2[at].astype(F32), sib_m2[at].astype(F32)),
                    hot,
                )
                rep[at] = jnp.where(mine | other, updated, 0.0).astype(BF16)

            blocks(k, body)
            for i in (2, 1, 3):
                g2_copy(k, i).start()

    def update(k):
        @pl.when(o == 1)
        def _():
            each(fwd_copy(k), "wait_recv")

        each(own_copy(k), "wait_recv")

        def body(at, hot):
            own = prod[at] + decoded(own_qi[at], own_si[:, cols[k]])
            gradient = jnp.where(belongs(g, WIDTHS[k]), hot, own)
            mst[at], m1[at], m2[at] = adamw(mst[at], m1[at], m2[at], gradient)

        blocks(k, body)

    def regather(k):
        @pl.when(o == 0)
        def _():
            for i in (1, 3, 2):
                g2_copy(k, i).wait_recv()
            rep_full[here, cols[k]] = (rep[here, cols[k]] + rep_slices[0, :, cols[k]]) + (
                rep_slices[1, :, cols[k]] + rep_slices[2, :, cols[k]]
            )
            for i in (2, 1, 3):
                g3_copy(k, i).start()

    def share(k):
        @pl.when(o == 0)
        def _():
            for i in (1, 3, 2):
                ag_wait(k, i, rep_full, s_g3)
            g4_copy(k).start()

    def finish(k):
        @pl.when(o == 1)
        def _():
            g4_copy(k).wait_recv()


    stages = [product, chip_sum, scatter, gather, replicate, regather, share, update, finish]
    order = sorted(
        (SPACING * k + i, -k * NEWEST, i, k) for k in range(count) for i in range(len(stages))
    )
    for _, _, i, k in order:
        stages[i](k)

    send_x.wait_send()
    for k in range(count):
        half = recv.at[0:15, :, cols[k]]
        remote(half, half, pair(s_a, k), sibling).wait_send()
        each(own_copy(k), "wait_send")
        sib_copy(k).wait_send()

        @pl.when(o == 1)
        def _():
            if k == 0:
                each(states, "wait_send")
            each(ring_copy(k), "wait_send")

        @pl.when(o == 0)
        def _():
            for i in (1, 2, 3):
                each(rs_copy(k, i), "wait_send")
                each(ag_copy(k, i), "wait_send")
                g2_copy(k, i).wait_send()
                g3_copy(k, i).wait_send()
            each(fwd_copy(k), "wait_send")
            g4_copy(k).wait_send()


def local(dy_rows, hidden_rows, row_counts, hot_owner, master, moment1, moment2):
    count = len(WIDTHS)
    dma = pltpu.SemaphoreType.DMA
    in_hbm = pl.BlockSpec(memory_space=pltpu.HBM)
    scalars = pl.BlockSpec(memory_space=pltpu.SMEM)
    return pl.pallas_call(
        kernel,
        name="expert_grad",
        out_shape=(
            pltpu.VMEM((1, 1, HID, WIN), F32),
            pltpu.VMEM((1, 1, HID, WIN), BF16),
            pltpu.VMEM((1, 1, HID, WIN), BF16),
            pltpu.VMEM((1, 1, HID, WIN), BF16),
        ),
        in_specs=[in_hbm, in_hbm, scalars, scalars, in_hbm, in_hbm, in_hbm],
        out_specs=(pl.BlockSpec(memory_space=pltpu.VMEM),) * 4,
        scratch_shapes=[
            pltpu.VMEM((16, 48, WIN), BF16),
            pltpu.VMEM((ROWS, HID), BF16),
            pltpu.VMEM((ROWS, HID), F32),
            pltpu.VMEM((ROWS, 4 * HID), F32),
            pltpu.VMEM((4 * HID, ROWS), BF16),
            pltpu.VMEM((ROWS // 2, 2 * HID), BF16),
            pltpu.VMEM((ROWS // 2, 2 * HID), BF16),
            pltpu.VMEM((3 * HID, WIN), F32),
            pltpu.VMEM((HID, WIN), I16),
            pltpu.VMEM((1, WIN), F32),
            pltpu.VMEM((HID, WIN), I16),
            pltpu.VMEM((1, WIN), F32),
            pltpu.VMEM((HID, WIN), F32),
            pltpu.VMEM((HID, WIN), I16),
            pltpu.VMEM((1, WIN), F32),
            pltpu.VMEM((HID, WIN), I16),
            pltpu.VMEM((1, WIN), F32),
            pltpu.VMEM((HID, WIN), I16),
            pltpu.VMEM((4, 1, WIN), F32),
            pltpu.VMEM((3, 32, WIN), I16),
            pltpu.VMEM((3, 1, WIN), F32),
            pltpu.VMEM((HID, WIN), I16),
            pltpu.VMEM((4, 1, WIN), F32),
            pltpu.VMEM((HID, WIN), F32),
            pltpu.VMEM((HID, WIN), BF16),
            pltpu.VMEM((HID, WIN), BF16),
            pltpu.VMEM((HID, WIN), BF16),
            pltpu.VMEM((3, 32, WIN), BF16),
            dma((4,)),
            dma((2, 3)),
            dma((2,)),
            dma((2, count)),
            dma((2, count, 2)),
            dma((2, count)),
            dma((2, count, 2)),
            dma((2, count, 3, 2)),
            dma((2, count, 3, 2)),
            dma((2, count, 2)),
            dma((2, count, 3)),
            dma((2, count, 3)),
            dma((2, count)),
        ],
        compiler_params=pltpu.CompilerParams(
            collective_id=0, has_side_effects=True, vmem_limit_bytes=52 * 2**20
        ),
        cost_estimate=pl.CostEstimate(
            flops=2 * 4 * HID * ROWS * WIN, bytes_accessed=16 * 2**20, transcendentals=HID * WIN
        ),
    )(dy_rows, hidden_rows, jnp.swapaxes(row_counts, 2, 3), hot_owner, master, moment1, moment2)


def solution(mesh):
    rows = P("group", "expert", None, None)
    return jax.shard_map(
        local,
        mesh=mesh,
        in_specs=(rows, rows, rows, P("expert"), rows, rows, rows),
        out_specs=(rows,) * 4,
        check_vma=False,
    )
```

time: 183 us -> 120 us (0.66)
  Pallas kernels: 175 us -> 113 us
  local copies, waits for them, and re-layouts: 7.14 us -> 4 us
    pallas_call x1, Pallas kernels: 175 us -> 113 us  [local(): pl.pallas_call(kernel, name='expert_grad', out_shape=(pltpu.VMEM((1, 1, H...]
    unnamed x11 -> x4, local copies, waits for them, and re-layouts: 7.14 us -> 4 us
where the time goes in v2:
time: 120 us; the launch traced here: 118 us
  Pallas kernels  113 us (94%)
  local copies, waits for them, and re-layouts  4 us (3%)
  between operations  1.29 us (1%)
    pallas_call x1, Pallas kernels, local(): pl.pallas_call(kernel, name='expert_grad', out_shape=(pltpu.VMEM((1, 1, H...  113 us
    unnamed x4, local copies, waits for them, and re-layouts  4 us

profile of v2, /device:TPU:7, one launch (start us, length us, event | category | flops | bytes accessed | tf_op | source)
XLA Modules:
  0.0 118.4 jit_solution(8780627243866106702)
XLA Ops:
  1.3 113.1 %expert_grad.1 = (f32[1,1,128,3584]{3,2,1,0:T(8,128)S(1)}, bf16[1,1,128,3584]{3,2,1,0:T(8,128)(2,1)S(1)}, bf16[1,1,128,3584]{3,2,1,0:T(8,128)(2,1)S(1)}, bf16[1,1,128,3584]{3,2,1,0:T(8,128)(2,1)S(1)}) custom-call(bf16[1,1,768,3584]{3,2,1,0:T(8,128)(2,1)} %dy.1, bf16[1,1,768,128]{3,2,1,0:T(8,128)(2,1)} %hid.1, s32[1,1,2,32]{3,2,1,0:T(2,128)} %bitcast.1, ...), custom_call_target="tpu_custom_call" | custom-call | flops 2818572288 | bytes 16777216 | tf_op jit(solution)/shard_map/expert_grad/pallas_call | solution.py:432
  114.4 1.2 %copy.15 = f32[1,1,128,3584]{3,2,1,0:T(8,128)} copy(f32[1,1,128,3584]{3,2,1,0:T(8,128)S(1)} %get-tuple-element.4) | data formatting | bytes 3670016
  115.6 0.9 copy.16
  116.5 0.9 copy.17
  117.4 0.9 copy.18

commit v3 on v2

--- a/solution.py
+++ b/solution.py
@@ -19,7 +19,8 @@
 bias_two = 1.0 - 0.95**10
 
 ROWS, HID, WIN, CAP = 768, 128, 3584, 24
-WIDTHS = (256,) * 14
+WIDTHS = (256,) * 12 + (512,)
+STATE_AT = 2
 SPACING = 1
 NEWEST = 1
 AHEAD = 2
@@ -84,8 +85,7 @@
         pltpu.make_async_copy(moment1.at[0, 0], m1, s_in.at[2]),
         pltpu.make_async_copy(moment2.at[0, 0], m2, s_in.at[3]),
     ]
-    for load in loads:
-        load.start()
+    loads[0].start()
 
     barrier = pltpu.get_barrier_semaphore()
     peers = [(g, plane(a, b) * 2 + p) for a, b in offsets]
@@ -146,10 +146,6 @@
     send_x.start()
     for k in range(1, min(AHEAD + 1, count)):
         rows_start(k)
-    @pl.when(o == 1)
-    def _():
-        for copy in states:
-            copy.start()
 
     left_f[...] = jnp.zeros_like(left_f)
 
@@ -257,6 +253,12 @@
         tiles(k, body)
         sib_copy(k).start()
         each(own_copy(k), "start")
+        if k == STATE_AT:
+            each(loads[1:], "start")
+
+            @pl.when(o == 1)
+            def _():
+                each(states, "start")
 
     def chip_sum(k):
         sib_copy(k).wait_recv()

time: 120 us -> 118 us (0.983)
  Pallas kernels: 113 us -> 111 us
    pallas_call x1, Pallas kernels: 113 us -> 111 us  [local(): pl.pallas_call(kernel, name='expert_grad', out_shape=(pltpu.VMEM((1, 1, H...]
where the time goes in v3:
time: 118 us; the launch traced here: 116 us
  Pallas kernels  111 us (94%)
  local copies, waits for them, and re-layouts  4 us (3%)
  between operations  1.29 us (1%)
    pallas_call x1, Pallas kernels, local(): pl.pallas_call(kernel, name='expert_grad', out_shape=(pltpu.VMEM((1, 1, H...  111 us
    unnamed x4, local copies, waits for them, and re-layouts  4 us

profile of v3, /device:TPU:7, one launch (start us, length us, event | category | flops | bytes accessed | tf_op | source)
XLA Modules:
  0.0 116.0 jit_solution(13543135841452271364)
XLA Ops:
  1.3 110.7 %expert_grad.1 = (f32[1,1,128,3584]{3,2,1,0:T(8,128)S(1)}, bf16[1,1,128,3584]{3,2,1,0:T(8,128)(2,1)S(1)}, bf16[1,1,128,3584]{3,2,1,0:T(8,128)(2,1)S(1)}, bf16[1,1,128,3584]{3,2,1,0:T(8,128)(2,1)S(1)}) custom-call(bf16[1,1,768,3584]{3,2,1,0:T(8,128)(2,1)} %dy.1, bf16[1,1,768,128]{3,2,1,0:T(8,128)(2,1)} %hid.1, s32[1,1,2,32]{3,2,1,0:T(2,128)} %bitcast.1, ...), custom_call_target="tpu_custom_call" | custom-call | flops 2818572288 | bytes 16777216 | tf_op jit(solution)/shard_map/expert_grad/pallas_call | solution.py:434
  112.0 1.2 %copy.15 = f32[1,1,128,3584]{3,2,1,0:T(8,128)} copy(f32[1,1,128,3584]{3,2,1,0:T(8,128)S(1)} %get-tuple-element.4) | data formatting | bytes 3670016
  113.2 0.9 copy.16
  114.1 0.9 copy.17
  115.1 0.9 copy.18
